TPU v7x, 256 devices: a whole 4x4x8 slice. The times are simulated.
256 devices in a mesh: tok: 8 (over x, core), code: 32 (over y, z).
Axes of the slice: x: 4, y: 4, z: 8, core: 2. Of those that a mesh axis runs over, the one named last changes fastest.
Arguments:
- latents: bfloat16 [2048, 256], P('tok'), may hold values from -240 to 240
- codebook: bfloat16 [262144, 256], P('code'), may hold values from -1.1953125 to 1.1953125
- cotangent: bfloat16 [2048, 256], P('tok'), may hold values from -6 to 6
- chosen: int32 [2048], P('tok'), may hold values from 0 to 262143
Outputs:
- latent_grad: float32 [2048, 256], P('tok')
- code_grad: float32 [262144, 256], P(('code', 'tok'))
All inputs are finite; a program needn't handle non-finite values.
Results may differ from a plain program's by a relative error of at most 0.004.
Values may be sent and summed in bfloat16 or wider, within the bound.
A program may use at most 64 MiB of HBM per device.

v0:
```python
import jax
import jax.numpy as jnp
from jax import lax
from jax.sharding import PartitionSpec as P


def shards(latents, codebook, cotangent, chosen):
    width = latents.shape[1]
    offset = lax.axis_index("code") * codebook.shape[0]
    tok_rows = latents.shape[0]
    code_rows = codebook.shape[0]
    block = min(2048, code_rows)
    blocks = codebook.reshape(code_rows // block, block, width)

    def logits_of(part):
        return jnp.dot(latents, part.T, preferred_element_type=jnp.float32)

    def first_pass(carry, part):
        top, total = carry
        scores = logits_of(part)
        newtop = jnp.maximum(top, jnp.max(scores, axis=1))
        total = total * jnp.exp(top - newtop) + jnp.sum(jnp.exp(scores - newtop[:, None]), axis=1)
        return ((newtop, total), None)

    start_top = jnp.full((tok_rows,), -1e30, jnp.float32)
    (local_top, local_total), unused = lax.scan(
        first_pass, (start_top, jnp.zeros((tok_rows,), jnp.float32)), blocks
    )
    top = lax.pmax(local_top, "code")
    total = lax.psum(local_total * jnp.exp(local_top - top), "code")

    def probs_of(part):
        return jnp.exp(logits_of(part) - top[:, None]) / total[:, None]

    def second_pass(carry, part):
        upstream = jnp.dot(cotangent, part.T, preferred_element_type=jnp.float32)
        return (carry + jnp.sum(probs_of(part) * upstream, axis=1), None)

    local_inner, unused = lax.scan(second_pass, jnp.zeros((tok_rows,), jnp.float32), blocks)
    inner = lax.psum(local_inner, "code")
    columns = lax.iota(jnp.int32, block)

    def third_pass(carry, item):
        part, index = item
        upstream = jnp.dot(cotangent, part.T, preferred_element_type=jnp.float32)
        dlogits = (probs_of(part) * (upstream - inner[:, None])).astype(jnp.bfloat16)
        carry = carry + jnp.dot(dlogits, part, preferred_element_type=jnp.float32)
        onehot = (chosen[:, None] == offset + index * block + columns[None, :]).astype(jnp.bfloat16)
        grads = jnp.dot(dlogits.T, latents, preferred_element_type=jnp.float32)
        grads = grads + jnp.dot(onehot.T, cotangent, preferred_element_type=jnp.float32)
        return (carry, grads)

    indices = lax.iota(jnp.int32, code_rows // block)
    local_latent, code_parts = lax.scan(
        third_pass, jnp.zeros((tok_rows, width), jnp.float32), (blocks, indices)
    )
    code_grad = lax.psum_scatter(
        code_parts.reshape(code_rows, width), "tok", scatter_dimension=0, tiled=True
    )
    latent_grad = lax.psum(local_latent, "code")
    return (latent_grad, code_grad)


def solution(mesh):
    in_specs = (P("tok", None), P("code", None), P("tok", None), P("tok"))
    out_specs = (P("tok", None), P(("code", "tok"), None))
    return jax.shard_map(shards, mesh=mesh, in_specs=in_specs, out_specs=out_specs, check_vma=False)
```

profile of v0, /device:TPU:2, one launch (start us, length us, event | category | flops | bytes accessed | tf_op | source)
XLA Modules:
  0.0 429.2 jit_solution(14318792894304877439)
XLA Ops:
  8.1 8.8 %while.37 = (s32[]{:T(128)}, f32[256]{0:T(256)S(1)}, f32[256]{0:T(256)S(1)}, bf16[4,2048,256]{2,1,0:T(8,128)(2,1)}, bf16[256,256]{1,0:T(8,128)(2,1)}, /*index=5*/s32[]{:T(128)}, s32[]{:T(128)}) while((s32[]{:T(128)}, f32[256]{0:T(256)S(1)}, f32[256]{0:T(256)S(1)}, bf16[4,2048,256]{2,1,0:T(8,128)(2,1)}, bf16[256,256]{1,0:T(8,128)(2,1)}, ...), condition=%wide.region_3.4_spmd.clone, body=%wide.region_0.3_spmd.clone.sunk | while | flops 270009600 | bytes 5387364 | solution.py:26
  8.1 1.8 fusion.71
  10.3 1.8 fusion.71
  12.5 1.8 fusion.71
  14.7 1.8 fusion.71
  16.9 77.9 %pmax.7 = f32[256]{0:T(256)S(1)} all-reduce(f32[256]{0:T(256)S(1)} %get-tuple-element.135), channel_id=1, replica_groups=mesh['tok'=8,'code'=32] {'code'}, use_global_device_ids=true, to_apply=%region_4.5 | all-reduce | flops 256 | bytes 2048 | tf_op jit(solution)/shard_map/pmax | solution.py:29
  94.8 69.6 %psum.21 = f32[256]{0:T(256)S(1)} all-reduce(f32[256]{0:T(256)S(1)} %exponential_multiply_fusion), channel_id=1, replica_groups=mesh['tok'=8,'code'=32] {'code'}, use_global_device_ids=true, to_apply=%region_5.6 | all-reduce | flops 256 | bytes 2048 | tf_op jit(solution)/shard_map/psum | solution.py:30
  164.5 14.5 %while.38 = (s32[]{:T(128)}, f32[256]{0:T(256)S(1)}, bf16[4,2048,256]{2,1,0:T(8,128)(2,1)}, bf16[256,256]{1,0:T(8,128)(2,1)}, f32[256]{0:T(256)S(1)}, /*index=5*...) while((s32[]{:T(128)}, f32[256]{0:T(256)S(1)}, ...), condition=%wide.region_8.9_spmd.clone, body=%wide.region_6.8_spmd.clone.sunk | while | flops 538968320 | bytes 6559863 | solution.py:39
  166.2 1.9 fusion.79
  168.1 1.7 fusion.78
  169.8 1.9 fusion.79
  173.5 1.9 fusion.79
  177.1 1.9 fusion.79
  179.0 71.7 %psum.22 = f32[256]{0:T(256)S(1)} all-reduce(f32[256]{0:T(256)S(1)} %get-tuple-element.137), channel_id=1, replica_groups=mesh['tok'=8,'code'=32] {'code'}, use_global_device_ids=true, to_apply=%region_9.10 | all-reduce | flops 256 | bytes 2048 | tf_op jit(solution)/shard_map/psum | solution.py:40
  250.7 30.6 %while.39 = (s32[]{:T(128)}, f32[256,256]{1,0:T(8,128)S(1)}, f32[4,2048,256]{2,1,0:T(8,128)}, bf16[4,2048,256]{2,1,0:T(8,128)(2,1)}, bf16[256,256]{1,0:T(8,128)(...) while((s32[]{:T(128)}, f32[256,256]{1,0:T(8,128)S(1)}, ...), condition=%wide.region_11.12_spmd.clone, body=%wide.region_10.11_spmd.clone.sunk | while | flops 1345980416 | bytes 35148044 | solution.py:54
  251.9 1.9 fusion.90
  256.2 2.2 fusion.93
  259.5 1.9 fusion.90
  263.9 2.1 fusion.93
  267.2 1.9 fusion.90
  271.5 2.1 fusion.93
  274.8 1.9 fusion.90
  279.2 2.2 fusion.93
  282.6 137.5 %all-reduce.2.cloned.1.call-done = f32[256,256]{1,0:T(8,128)} async-done(((f32[256,256]{1,0:T(8,128)}), f32[256,256]{1,0:T(8,128)}) %all-reduce.2.cloned.1.call-update) | async-done | bytes 262160 | tf_op jit(solution)/shard_map/psum | solution.py:60
  (78 shorter events, 21.8 us)
Async XLA Ops:
  8.0 412.1 %all-reduce.2.cloned.1.call-start = ((), (), s32[]{:S(2)}) async-start(), calls=%async_computation.1 | async-start | bytes 524288 | tf_op jit(solution)/shard_map/psum | solution.py:60
  8.1 156.4 %copy-start.1 = (bf16[256,256]{1,0:T(8,128)(2,1)S(1)}, bf16[256,256]{1,0:T(8,128)(2,1)}, u32[]{:S(2)}) copy-start(bf16[256,256]{1,0:T(8,128)(2,1)} %param.12) | copy-start | bytes 393220
  164.5 86.2 %copy-start.4 = (s32[256]{0:T(256)S(1)}, s32[256]{0:T(256)}, u32[]{:S(2)}) copy-start(s32[256]{0:T(256)} %param.13) | copy-start | bytes 3076
  251.8 2.5 copy-start
  254.9 0.9 copy-start.2
  259.5 2.5 copy-start
  262.5 0.9 copy-start.2
  267.1 2.5 copy-start
  270.2 0.9 copy-start.2
  274.8 2.5 copy-start
  277.8 0.9 copy-start.2
  281.3 0.7 copy-start.3
  282.0 138.0 %reduce-scatter.2.cloned.1.call-start = ((), (), s32[]{:S(2)}) async-start(), calls=%async_computation.2 | async-start | bytes 9437184 | tf_op jit(solution)/shard_map/reduce_scatter | solution.py:57
Sparse Core Ops, SparseCore 0:
  282.2 137.8 all-reduce.1
Sparse Core Ops, SparseCore 1:
  285.6 46.1 reduce-scatter.1
where the time goes:
time: 430 us; the launch traced here: 429 us
  blocking collectives  219 us (51%)
  waiting for transfers between devices  138 us (32%)
  matrix products  43.3 us (10%)
  between operations  15.5 us (4%)
  local copies, waits for them, and re-layouts  8.74 us (2%)
    psum x1, waiting for transfers between devices, shards(): latent_grad = lax.psum(local_latent, 'code')  137 us
    pmax x1, blocking collectives, shards(): top = lax.pmax(local_top, 'code')  77.9 us
    psum x1, blocking collectives, shards(): inner = lax.psum(local_inner, 'code')  71.7 us
    psum x1, blocking collectives, shards(): total = lax.psum(local_total * jnp.exp(local_top - top), 'code')  69.6 us
    dot_general x12, matrix products, logits_of(): return jnp.dot(latents, part.T, preferred_element_type=jnp.float32)  21.4 us
    dot_general x4, matrix products, third_pass(): jnp.dot(onehot.T, cotangent, preferred_element_type=jnp.float32)  8.6 us
  transfers between devices with their start and end apart: 2, of which 1 were waited for; matrix products, arithmetic and copies ran while one was open for 0% of the time, Pallas kernels for 0%

commit v1 on v0

v1 whole, which is shorter than its diff:
```python
import jax
import jax.numpy as jnp
from jax import lax
from jax.experimental import pallas as pl
from jax.experimental.pallas import tpu as pltpu
from jax.sharding import PartitionSpec as P

MESH = pl.DeviceIdType.MESH
F32, BF16 = jnp.float32, jnp.bfloat16
NX, NY, NZ = 4, 4, 8
PLANE = NY * NZ
T = 256
D = 256
CODES = 8192
OWN = CODES // NX
HALF = OWN // 2
ROWS = 256

SHIFTS = sorted(
    ((dy, dz) for dy in range(NY) for dz in range(NZ) if (dy, dz) != (0, 0)),
    key=lambda s: -(min(s[0], NY - s[0]) + min(s[1], NZ - s[1])),
)
LOG2E = 1.4426950408889634
PARTS = (2048, 2048, 4096)
STEP = 1024


def nt(a, b):
    return lax.dot_general(a, b, (((1,), (1,)), ((), ())), preferred_element_type=F32)


def tn(a, b):
    return lax.dot_general(a, b, (((0,), (0,)), ((), ())), preferred_element_type=F32)


def nn(a, b):
    return jnp.dot(a, b, preferred_element_type=F32)


def row(v):
    return jnp.concatenate([v[0:1], v[1:2]], axis=1)


def pair(v):
    return jnp.concatenate([v[:, :128], v[:, 128:]], axis=0)


def fold8(v):
    return v.reshape(v.shape[0] // 8, 8, v.shape[1])


def rank_of(y, z):
    late = jnp.where(z < 5, z, jnp.where(z == 7, 5, z + 1))
    return late * NY + y


def code_of(rank):
    y, late = rank & (NY - 1), rank >> 2
    z = jnp.where(late < 5, late, jnp.where(late == 5, 7, late - 1))
    return y * NZ + z


def kernel(
    lat_hbm, cot_hbm, cho_hbm, cb_hbm, ag, cg_out,
    cb, lat, cot, cho, lq, uu, lb, ub, stats, fin, acc_a, acc_b,
    rs_out, rs_in, ag_own, cacc, cx_out, cx_in, cg,
    cb_sem, own_sem, gat_send, gat_recv, st_send, st_recv, fin_send, fin_recv,
    rs_send, rs_recv, ag_send, ag_recv, cx_send, cx_recv, out_sem, ready_sem,
):
    tok, code = lax.axis_index("tok"), lax.axis_index("code")
    x, c = tok >> 1, tok & 1
    y, z = code >> 3, code & (NZ - 1)

    x_peers = [((((x + d) & (NX - 1)) << 1) + c, code) for d in range(1, NX)]
    plane_codes = [(((y + dy) & (NY - 1)) << 3) + ((z + dz) & (NZ - 1)) for dy, dz in SHIFTS]
    plane = [(tok, p) for p in plane_codes]
    other = (tok ^ 1, code)

    def remote(src, dst, send, recv, to):
        return pltpu.make_async_remote_copy(
            src_ref=src, dst_ref=dst, send_sem=send, recv_sem=recv, device_id=to, device_id_type=MESH
        )

    def all_of(ref, send, recv):
        return remote(ref, ref, send, recv, other)

    own = [
        pltpu.make_async_copy(lat_hbm, lat.at[0], own_sem.at[0]),
        pltpu.make_async_copy(cot_hbm, cot.at[0], own_sem.at[1]),
        pltpu.make_async_copy(cho_hbm, cho.at[0], own_sem.at[2]),
    ]
    starts = [sum(PARTS[:k]) for k in range(len(PARTS))]
    loads = [
        pltpu.make_async_copy(cb_hbm.at[pl.ds(at, n)], cb.at[pl.ds(at, n)], cb_sem.at[k])
        for k, (at, n) in enumerate(zip(starts, PARTS))
    ]
    own[0].start()
    for load in loads:
        load.start()
    own[1].start()
    own[2].start()

    rank = rank_of(y, z)

    def tell(sem):
        def one(r, carry):
            pl.semaphore_signal(sem, inc=1, device_id=(tok, code_of(r)), device_id_type=MESH)
            return carry

        return one

    with jax.named_scope("greet"):
        barrier = pltpu.get_barrier_semaphore()
        near = x_peers + [other]
        for p in near:
            pl.semaphore_signal(barrier, inc=1, device_id=p, device_id_type=MESH)
        lax.fori_loop(rank + 1, PLANE, tell(barrier), 0)

    def logits(k, top):
        rows = pl.ds(starts[k], PARTS[k])
        loads[k].wait()
        scores = nt(cb[rows, :], lat[0]) * LOG2E
        lq[rows, :] = scores
        return jnp.maximum(top, jnp.max(fold8(scores), axis=0))

    with jax.named_scope("own_wait"):
        own[0].wait()
    with jax.named_scope("logits_first"):
        top8 = logits(0, jnp.full((8, T), -jnp.inf, F32))

    with jax.named_scope("entry"):
        pl.semaphore_wait(barrier, len(near) + rank)
    for d in (2, 1, 3):
        to = x_peers[d - 1]
        remote(lat_hbm, lat.at[d], gat_send.at[0], gat_recv.at[0], to).start()
        remote(cot_hbm, cot.at[d], gat_send.at[1], gat_recv.at[1], to).start()
        remote(cho_hbm, cho.at[d], gat_send.at[2], gat_recv.at[2], to).start()
    lax.fori_loop(0, rank, tell(ready_sem), 0)

    with jax.named_scope("logits_rest"):
        for k in range(1, len(PARTS)):
            top8 = logits(k, top8)
        top = jnp.max(top8, axis=0, keepdims=True)
        own[1].wait()
        own[2].wait()

    with jax.named_scope("stats"):

        def stats_step(k, carry):
            total8, inner8 = carry
            rows = pl.ds(pl.multiple_of(k * STEP, STEP), STEP)
            up = nt(cb[rows, :], cot[0])
            uu[rows, :] = up
            q = jnp.exp2(lq[rows, :] - top)
            lq[rows, :] = q
            total8 = total8 + jnp.sum(fold8(q), axis=0)
            inner8 = inner8 + jnp.sum(fold8(q * up), axis=0)
            return total8, inner8

        zero8 = jnp.zeros((8, T), F32)
        total8, inner8 = lax.fori_loop(0, CODES // STEP, stats_step, (zero8, zero8), unroll=True)
        total = jnp.sum(total8, axis=0, keepdims=True)
        inner = jnp.sum(inner8, axis=0, keepdims=True)
        stats[0, 0] = pair(top)
        stats[0, 1] = pair(total)
        stats[0, 2] = pair(inner)
    with jax.named_scope("ready"):

        @pl.when(rank < PLANE - 1)
        def later_ones():
            pl.semaphore_wait(ready_sem, PLANE - 1 - rank)

    for k, p in enumerate(plane):
        remote(stats.at[0], stats.at[k + 1], st_send, st_recv, p).start()
    inner_loc = inner / total

    with jax.named_scope("sums"):
        acc_a[...] = jnp.zeros_like(acc_a)
        acc_b[...] = jnp.zeros_like(acc_b)

        def sums_step(k, carry):
            rows = pl.ds(pl.multiple_of(k * STEP, STEP), STEP)
            q = lq[rows, :]
            part = cb[rows, :]
            acc_a[...] += tn(part, (q * (uu[rows, :] - inner_loc)).astype(BF16))
            acc_b[...] += tn(part, q.astype(BF16))
            return carry

        lax.fori_loop(0, CODES // STEP, sums_step, 0, unroll=True)

    with jax.named_scope("stats_wait"):
        all_of(stats.at[pl.ds(1, PLANE - 1)], st_send, st_recv).wait_recv()
    with jax.named_scope("combine"):
        tops = stats[:, 0]
        big = jnp.max(tops, axis=0)
        weights = jnp.exp2(tops - big)
        whole = jnp.sum(weights * stats[:, 1], axis=0)
        scale = 1.0 / whole
        mean = jnp.sum(weights * stats[:, 2], axis=0) * scale
        fin[0, 0] = big
        fin[0, 1] = scale
        fin[0, 2] = mean
        own_scale = row(jnp.exp2(pair(top) - big) * scale)
        own_inner = row(mean)
        part = own_scale * (acc_a[...] - (own_inner - inner_loc) * acc_b[...])
        rs_out[...] = jnp.concatenate(
            [part[:, :128].reshape(PLANE, 8, 128), part[:, 128:].reshape(PLANE, 8, 128)], axis=1
        ).astype(BF16)
    for k, p in enumerate(plane):
        remote(rs_out.at[plane_codes[k]], rs_in.at[k], rs_send, rs_recv, p).start()
    for d in (2, 1, 3):
        remote(fin.at[0], fin.at[d], fin_send, fin_recv, x_peers[d - 1]).start()

    base = pl.multiple_of(x * OWN, OWN)

    def scores_of_codes():
        with jax.named_scope("gather_wait"):
            all_of(lat.at[pl.ds(1, NX - 1)], gat_send.at[0], gat_recv.at[0]).wait_recv()
            all_of(cot.at[pl.ds(1, NX - 1)], gat_send.at[1], gat_recv.at[1]).wait_recv()
            all_of(cho.at[pl.ds(1, NX - 1)], gat_send.at[2], gat_recv.at[2]).wait_recv()
        with jax.named_scope("code_scores"):
            codes = pl.ds(base, OWN)
            for g in range(1, NX):
                lb[g - 1] = nt(cb[codes, :], lat[g]) * LOG2E
                ub[g - 1] = nt(cb[codes, :], cot[g])
        with jax.named_scope("chosen"):
            ids = lax.broadcasted_iota(jnp.int32, (ROWS, T), 0)
            all_cot = cot[...].reshape(NX * T, D)

            def chosen_step(k, carry):
                at = pl.multiple_of(k * ROWS, ROWS)
                first = code * CODES + base + at
                hot = [jnp.where(ids == cho[g] - first, 1.0, 0.0).astype(BF16) for g in range(NX)]
                cacc[pl.ds(at, ROWS), :] = nn(jnp.concatenate(hot, axis=1), all_cot)
                return carry

            lax.fori_loop(0, OWN // ROWS, chosen_step, 0, unroll=True)

    pl.when(z < NZ // 2)(scores_of_codes)

    with jax.named_scope("rs_wait"):
        all_of(rs_in, rs_send, rs_recv).wait_recv()
    with jax.named_scope("latent_sum"):
        mine = rs_out[code].astype(F32) + jnp.sum(rs_in[...].astype(F32), axis=0)
        ag_own[...] = mine.astype(BF16)
    for p in plane:
        remote(ag_own, ag.at[code], ag_send, ag_recv, p).start()
    ag_local = pltpu.make_async_copy(ag_own, ag.at[code], out_sem.at[1])
    ag_local.start()

    pl.when(z >= NZ // 2)(scores_of_codes)

    with jax.named_scope("fin_wait"):
        all_of(fin.at[pl.ds(1, NX - 1)], fin_send, fin_recv).wait_recv()

    with jax.named_scope("code_grads"):
        bigs = [row(fin[g, 0]) for g in range(NX)]
        scales = [row(fin[g, 1]) for g in range(NX)]
        means = [row(fin[g, 2]) for g in range(NX)]
        all_lat = lat[...].reshape(NX * T, D)

        def grads_of(half, k):
            at = pl.multiple_of(half * HALF + k * ROWS, ROWS)
            rows = pl.ds(at, ROWS)
            own_rows = pl.ds(pl.multiple_of(base + at, ROWS), ROWS)
            dlogits = [((lq[own_rows, :] * own_scale) * (uu[own_rows, :] - own_inner)).astype(BF16)]
            for g in range(1, NX):
                probs = jnp.exp2(lb[g - 1, rows, :] - bigs[g]) * scales[g]
                dlogits.append((probs * (ub[g - 1, rows, :] - means[g])).astype(BF16))
            return cacc[rows, :] + nn(jnp.concatenate(dlogits, axis=1), all_lat)

        def other_step(k, carry):
            cx_out[pl.ds(pl.multiple_of(k * ROWS, ROWS), ROWS), :] = grads_of(1 - c, k).astype(BF16)
            return carry

        lax.fori_loop(0, HALF // ROWS, other_step, 0, unroll=True)
        to_other = remote(cx_out, cx_in, cx_send, cx_recv, other)
        to_other.start()

        def own_step(k, carry):
            cg[pl.ds(pl.multiple_of(k * ROWS, ROWS), ROWS), :] = grads_of(c, k)
            return carry

        lax.fori_loop(0, HALF // ROWS, own_step, 0, unroll=True)

    with jax.named_scope("core_wait"):
        to_other.wait_recv()
    with jax.named_scope("code_out"):
        cg[...] += cx_in[...].astype(F32)
        out_cg = pltpu.make_async_copy(cg, cg_out, out_sem.at[0])
        out_cg.start()

    with jax.named_scope("drain"):
        to_other.wait_send()
        all_of(lat.at[pl.ds(1, NX - 1)], gat_send.at[0], gat_recv.at[0]).wait_send()
        all_of(cot.at[pl.ds(1, NX - 1)], gat_send.at[1], gat_recv.at[1]).wait_send()
        all_of(cho.at[pl.ds(1, NX - 1)], gat_send.at[2], gat_recv.at[2]).wait_send()
        all_of(stats.at[pl.ds(1, PLANE - 1)], st_send, st_recv).wait_send()
        all_of(fin.at[pl.ds(1, NX - 1)], fin_send, fin_recv).wait_send()
        all_of(rs_in, rs_send, rs_recv).wait_send()
        ag_local.wait()
        out_cg.wait()

    with jax.named_scope("ag_wait"):
        all_of(rs_in, ag_send, ag_recv).wait_send()
        all_of(rs_in, ag_send, ag_recv).wait_recv()


def finish(ag, cg, lg_out, cg_out, ag_v, lg_v, cg_v, sem):
    load = pltpu.make_async_copy(ag, ag_v, sem.at[0])
    load.start()
    n = cg_v.shape[0]
    pieces = [pl.ds(k * (HALF // n), HALF // n) for k in range(n)]
    moves = [pltpu.make_async_copy(cg.at[p], cg_v.at[k], sem.at[2 + k]) for k, p in enumerate(pieces)]
    for move in moves:
        move.start()
    load.wait()
    full = ag_v[...].astype(F32)
    lg_v[pl.ds(0, 128), :] = full[:, :8, :].reshape(D, 128).T
    lg_v[pl.ds(128, 128), :] = full[:, 8:, :].reshape(D, 128).T
    store = pltpu.make_async_copy(lg_v, lg_out, sem.at[1])
    store.start()
    stores = [pltpu.make_async_copy(cg_v.at[k], cg_out.at[p], sem.at[2 + n + k]) for k, p in enumerate(pieces)]
    for move, out in zip(moves, stores):
        move.wait()
        out.start()
    store.wait()
    for out in stores:
        out.wait()


def shards(latents, codebook, cotangent, chosen):
    any_space = pl.BlockSpec(memory_space=pl.ANY)
    dma = pltpu.SemaphoreType.DMA
    gathered, code_grad = pl.pallas_call(
        kernel,
        out_shape=(
            jax.ShapeDtypeStruct((PLANE, 16, 128), BF16),
            jax.ShapeDtypeStruct((HALF, D), F32),
        ),
        in_specs=[any_space] * 4,
        out_specs=(any_space, any_space),
        scratch_shapes=[
            pltpu.VMEM((CODES, D), BF16),
            pltpu.VMEM((NX, T, D), BF16),
            pltpu.VMEM((NX, T, D), BF16),
            pltpu.VMEM((NX, 1, T), jnp.int32),
            pltpu.VMEM((CODES, T), F32),
            pltpu.VMEM((CODES, T), F32),
            pltpu.VMEM((NX - 1, OWN, T), F32),
            pltpu.VMEM((NX - 1, OWN, T), F32),
            pltpu.VMEM((PLANE, 3, 2, 128), F32),
            pltpu.VMEM((NX, 3, 2, 128), F32),
            pltpu.VMEM((D, T), F32),
            pltpu.VMEM((D, T), F32),
            pltpu.VMEM((PLANE, 16, 128), BF16),
            pltpu.VMEM((PLANE - 1, 16, 128), BF16),
            pltpu.VMEM((16, 128), BF16),
            pltpu.VMEM((OWN, D), F32),
            pltpu.VMEM((HALF, D), BF16),
            pltpu.VMEM((HALF, D), BF16),
            pltpu.VMEM((HALF, D), F32),
            dma((len(PARTS),)),
            dma((3,)),
            dma((3,)), dma((3,)),
            dma, dma,
            dma, dma,
            dma, dma,
            dma, dma,
            dma, dma,
            dma((2,)),
            pltpu.SemaphoreType.REGULAR,
        ],
        compiler_params=pltpu.CompilerParams(
            collective_id=0, has_side_effects=True, vmem_limit_bytes=56 * 2**20
        ),
        cost_estimate=pl.CostEstimate(
            flops=20 * T * D * CODES, bytes_accessed=8 * 2**20, transcendentals=2 * T * CODES
        ),
    )(latents, cotangent, chosen.reshape(1, T), codebook)
    return pl.pallas_call(
        finish,
        out_shape=(jax.ShapeDtypeStruct((T, D), F32), jax.ShapeDtypeStruct((HALF, D), F32)),
        in_specs=[any_space] * 2,
        out_specs=(any_space, any_space),
        scratch_shapes=[
            pltpu.VMEM((PLANE, 16, 128), BF16),
            pltpu.VMEM((T, D), F32),
            pltpu.VMEM((4, HALF // 4, D), F32),
            dma((10,)),
        ],
    )(gathered, code_grad)


def solution(mesh):
    in_specs = (P("tok", None), P("code", None), P("tok", None), P("tok"))
    out_specs = (P("tok", None), P(("code", "tok"), None))
    return jax.shard_map(shards, mesh=mesh, in_specs=in_specs, out_specs=out_specs, check_vma=False)
```

time: 430 us -> 34.1 us (0.08)
  blocking collectives: 219 us -> 0 us
  waiting for transfers between devices: 138 us -> 0 us
  matrix products: 43.3 us -> 0 us
  Pallas kernels: 0 us -> 33.2 us
  between operations: 15.5 us -> 0.8 us
  local copies, waits for them, and re-layouts: 8.74 us -> 0 us
    psum x2 -> x0, blocking collectives: 141 us -> none  [the longest x1 71.7 us: shards(): inner = lax.psum(local_inner, 'code')]
    psum x1 -> x0, waiting for transfers between devices: 137 us -> none  [shards(): latent_grad = lax.psum(local_latent, 'code')]
    pmax x1 -> x0, blocking collectives: 77.9 us -> none  [shards(): top = lax.pmax(local_top, 'code')]
    dot_general x32 -> x0, matrix products: 43.3 us -> none  [the longest x12 21.4 us: logits_of(): return jnp.dot(latents, part.T, preferred_element_type=jnp.float32)]
    pallas_call x0 -> x2, Pallas kernels: none -> 33.2 us  [the longest x1 31.1 us: shards(): pl.pallas_call(kernel, out_shape=(jax.ShapeDtypeStruct((PLANE, 16, 128),...]
  transfers between devices with their start and end apart: 2 -> 0, of which waited for: 1 -> 0; matrix products, arithmetic and copies ran while one was open for 0% -> 0% of each run, Pallas kernels for 0% -> 0%
where the time goes in v1:
time: 34.1 us; the launch traced here: 34 us
  Pallas kernels  33.2 us (97%)
  between operations  0.8 us (2%)
    pallas_call x1, Pallas kernels, shards(): pl.pallas_call(kernel, out_shape=(jax.ShapeDtypeStruct((PLANE, 16, 128),...  31.1 us
    pallas_call x1, Pallas kernels, shards(): pl.pallas_call(finish, out_shape=(jax.ShapeDtypeStruct((T, D), F32), jax....  2.14 us

profile of v1, /device:TPU:2, one launch (start us, length us, event | category | flops | bytes accessed | tf_op | source)
XLA Modules:
  0.0 34.0 jit_solution(1840161217761531237)
XLA Ops:
  0.6 31.1 %shard_map.59 = (bf16[32,16,128]{2,1,0:T(8,128)(2,1)}, f32[1024,256]{1,0:T(8,128)}) custom-call(bf16[256,256]{1,0:T(8,128)(2,1)} %lat_hbm.1, bf16[256,256]{1,0:T(8,128)(2,1)} %cot_hbm.1, s32[1,256]{1,0:T(1,128)} %bitcast.1, bf16[8192,256]{1,0:T(8,128)(2,1)} %cb_hbm.1), custom_call_target="tpu_custom_call" | custom-call | flops 10737418240 | bytes 8388608 | tf_op jit(solution)/shard_map/pallas_call | solution.py:335
  31.7 2.1 %shard_map.60 = (f32[256,256]{1,0:T(8,128)}, f32[1024,256]{1,0:T(8,128)}) custom-call(bf16[32,16,128]{2,1,0:T(8,128)(2,1)} %get-tuple-element.4.ag, f32[1024,256]{1,0:T(8,128)} %get-tuple-element.5.cg), custom_call_target="tpu_custom_call" | custom-call | tf_op jit(solution)/shard_map/pallas_call | solution.py:381

commit v2 on v1

--- a/solution.py
+++ b/solution.py
@@ -21,7 +21,7 @@
     key=lambda s: -(min(s[0], NY - s[0]) + min(s[1], NZ - s[1])),
 )
 LOG2E = 1.4426950408889634
-PARTS = (2048, 2048, 4096)
+PARTS = (1024, 3072, 4096)
 STEP = 1024
 
 
@@ -61,11 +61,11 @@
 
 
 def kernel(
-    lat_hbm, cot_hbm, cho_hbm, cb_hbm, ag, cg_out,
+    lat_hbm, cot_hbm, cho_hbm, cb_hbm, ag, cg,
     cb, lat, cot, cho, lq, uu, lb, ub, stats, fin, acc_a, acc_b,
-    rs_out, rs_in, ag_own, cacc, cx_out, cx_in, cg,
+    rs_out, rs_in, coef, ag_own, cacc, cx_out, cx_in,
     cb_sem, own_sem, gat_send, gat_recv, st_send, st_recv, fin_send, fin_recv,
-    rs_send, rs_recv, ag_send, ag_recv, cx_send, cx_recv, out_sem, ready_sem,
+    rs_send, rs_recv, ag_send, ag_recv, cx_send, cx_recv, ready_sem,
 ):
     tok, code = lax.axis_index("tok"), lax.axis_index("code")
     x, c = tok >> 1, tok & 1
@@ -117,16 +117,21 @@
         lax.fori_loop(rank + 1, PLANE, tell(barrier), 0)
 
     def logits(k, top):
-        rows = pl.ds(starts[k], PARTS[k])
         loads[k].wait()
-        scores = nt(cb[rows, :], lat[0]) * LOG2E
-        lq[rows, :] = scores
-        return jnp.maximum(top, jnp.max(fold8(scores), axis=0))
+
+        def step(j, top):
+            rows = pl.ds(pl.multiple_of(starts[k] + j * STEP, STEP), STEP)
+            scores = nt(cb[rows, :], lat[0]) * LOG2E
+            lq[rows, :] = scores
+            return jnp.maximum(top, jnp.max(fold8(scores), axis=0))
+
+        return lax.fori_loop(0, PARTS[k] // STEP, step, top, unroll=True)
 
     with jax.named_scope("own_wait"):
         own[0].wait()
     with jax.named_scope("logits_first"):
         top8 = logits(0, jnp.full((8, T), -jnp.inf, F32))
+        top8 = logits(1, top8)
 
     with jax.named_scope("entry"):
         pl.semaphore_wait(barrier, len(near) + rank)
@@ -138,8 +143,7 @@
     lax.fori_loop(0, rank, tell(ready_sem), 0)
 
     with jax.named_scope("logits_rest"):
-        for k in range(1, len(PARTS)):
-            top8 = logits(k, top8)
+        top8 = logits(2, top8)
         top = jnp.max(top8, axis=0, keepdims=True)
         own[1].wait()
         own[2].wait()
@@ -161,18 +165,21 @@
         total8, inner8 = lax.fori_loop(0, CODES // STEP, stats_step, (zero8, zero8), unroll=True)
         total = jnp.sum(total8, axis=0, keepdims=True)
         inner = jnp.sum(inner8, axis=0, keepdims=True)
-        stats[0, 0] = pair(top)
-        stats[0, 1] = pair(total)
-        stats[0, 2] = pair(inner)
-    with jax.named_scope("ready"):
-
-        @pl.when(rank < PLANE - 1)
-        def later_ones():
-            pl.semaphore_wait(ready_sem, PLANE - 1 - rank)
-
-    for k, p in enumerate(plane):
-        remote(stats.at[0], stats.at[k + 1], st_send, st_recv, p).start()
-    inner_loc = inner / total
+        inner_loc = inner / total
+        stats[0, 0] = pair(top + jnp.log(total) * LOG2E)
+        stats[0, 1] = pair(inner_loc)
+
+    def send_stats():
+        with jax.named_scope("ready"):
+
+            @pl.when(rank < PLANE - 1)
+            def later_ones():
+                pl.semaphore_wait(ready_sem, PLANE - 1 - rank)
+
+        for k, p in enumerate(plane):
+            remote(stats.at[0], stats.at[k + 1], st_send, st_recv, p).start()
+
+    pl.when(z >= NZ // 2)(send_stats)
 
     with jax.named_scope("sums"):
         acc_a[...] = jnp.zeros_like(acc_a)
@@ -188,26 +195,33 @@
 
         lax.fori_loop(0, CODES // STEP, sums_step, 0, unroll=True)
 
+        for i, acc in enumerate((acc_a, acc_b)):
+            whole = acc[...] * (1.0 / total)
+            rs_out[:, i] = jnp.concatenate(
+                [whole[:, :128].reshape(PLANE, 8, 128), whole[:, 128:].reshape(PLANE, 8, 128)], axis=1
+            ).astype(BF16)
+    pl.when(z < NZ // 2)(send_stats)
+    for k, p in enumerate(plane):
+        remote(rs_out.at[plane_codes[k]], rs_in.at[k + 1], rs_send, rs_recv, p).start()
+    rs_local = pltpu.make_async_copy(rs_out.at[code], rs_in.at[0], own_sem.at[3])
+    rs_local.start()
+
     with jax.named_scope("stats_wait"):
         all_of(stats.at[pl.ds(1, PLANE - 1)], st_send, st_recv).wait_recv()
     with jax.named_scope("combine"):
-        tops = stats[:, 0]
-        big = jnp.max(tops, axis=0)
-        weights = jnp.exp2(tops - big)
-        whole = jnp.sum(weights * stats[:, 1], axis=0)
-        scale = 1.0 / whole
-        mean = jnp.sum(weights * stats[:, 2], axis=0) * scale
-        fin[0, 0] = big
-        fin[0, 1] = scale
-        fin[0, 2] = mean
-        own_scale = row(jnp.exp2(pair(top) - big) * scale)
+        logs = stats[:, 0]
+        inners = stats[:, 1]
+        big = jnp.max(logs, axis=0)
+        weights = jnp.exp2(logs - big)
+        whole = jnp.sum(weights, axis=0)
+        weights = weights * (1.0 / whole)
+        mean = jnp.sum(weights * inners, axis=0)
+        fin[0, 0] = big + jnp.log(whole) * LOG2E
+        fin[0, 1] = mean
+        coef[:, 0] = weights
+        coef[:, 1] = weights * (mean - inners)
+        own_scale = row(weights[0]) * (1.0 / total)
         own_inner = row(mean)
-        part = own_scale * (acc_a[...] - (own_inner - inner_loc) * acc_b[...])
-        rs_out[...] = jnp.concatenate(
-            [part[:, :128].reshape(PLANE, 8, 128), part[:, 128:].reshape(PLANE, 8, 128)], axis=1
-        ).astype(BF16)
-    for k, p in enumerate(plane):
-        remote(rs_out.at[plane_codes[k]], rs_in.at[k], rs_send, rs_recv, p).start()
     for d in (2, 1, 3):
         remote(fin.at[0], fin.at[d], fin_send, fin_recv, x_peers[d - 1]).start()
 
@@ -236,27 +250,34 @@
 
             lax.fori_loop(0, OWN // ROWS, chosen_step, 0, unroll=True)
 
-    pl.when(z < NZ // 2)(scores_of_codes)
+    pl.when(z < NZ // 2 - 1)(scores_of_codes)
 
     with jax.named_scope("rs_wait"):
-        all_of(rs_in, rs_send, rs_recv).wait_recv()
+        rs_local.wait()
+        all_of(rs_in.at[pl.ds(1, PLANE - 1)], rs_send, rs_recv).wait_recv()
     with jax.named_scope("latent_sum"):
-        mine = rs_out[code].astype(F32) + jnp.sum(rs_in[...].astype(F32), axis=0)
-        ag_own[...] = mine.astype(BF16)
-    for p in plane:
-        remote(ag_own, ag.at[code], ag_send, ag_recv, p).start()
-    ag_local = pltpu.make_async_copy(ag_own, ag.at[code], out_sem.at[1])
-    ag_local.start()
-
-    pl.when(z >= NZ // 2)(scores_of_codes)
+        parts = rs_in[...].astype(F32).reshape(PLANE, 2, 2, 8, 128)
+        by_a = coef[:, 0].reshape(PLANE, 2, 1, 128)
+        by_b = coef[:, 1].reshape(PLANE, 2, 1, 128)
+        mine = jnp.sum(by_a * parts[:, 0] - by_b * parts[:, 1], axis=0)
+        ag_own[...] = mine.reshape(16, 128).astype(BF16)
+        ag[code] = ag_own[...]
+
+    def ag_to(r, carry):
+        remote(ag_own, ag.at[code], ag_send, ag_recv, (tok, code_of(r))).start()
+        return carry
+
+    lax.fori_loop(0, rank, ag_to, 0)
+    lax.fori_loop(rank + 1, PLANE, ag_to, 0)
+
+    pl.when(z >= NZ // 2 - 1)(scores_of_codes)
 
     with jax.named_scope("fin_wait"):
         all_of(fin.at[pl.ds(1, NX - 1)], fin_send, fin_recv).wait_recv()
 
     with jax.named_scope("code_grads"):
-        bigs = [row(fin[g, 0]) for g in range(NX)]
-        scales = [row(fin[g, 1]) for g in range(NX)]
-        means = [row(fin[g, 2]) for g in range(NX)]
+        logs_of = [row(fin[g, 0]) for g in range(NX)]
+        means = [row(fin[g, 1]) for g in range(NX)]
         all_lat = lat[...].reshape(NX * T, D)
 
         def grads_of(half, k):
@@ -265,7 +286,7 @@
             own_rows = pl.ds(pl.multiple_of(base + at, ROWS), ROWS)
             dlogits = [((lq[own_rows, :] * own_scale) * (uu[own_rows, :] - own_inner)).astype(BF16)]
             for g in range(1, NX):
-                probs = jnp.exp2(lb[g - 1, rows, :] - bigs[g]) * scales[g]
+                probs = jnp.exp2(lb[g - 1, rows, :] - logs_of[g])
                 dlogits.append((probs * (ub[g - 1, rows, :] - means[g])).astype(BF16))
             return cacc[rows, :] + nn(jnp.concatenate(dlogits, axis=1), all_lat)
 
@@ -287,8 +308,6 @@
         to_other.wait_recv()
     with jax.named_scope("code_out"):
         cg[...] += cx_in[...].astype(F32)
-        out_cg = pltpu.make_async_copy(cg, cg_out, out_sem.at[0])
-        out_cg.start()
 
     with jax.named_scope("drain"):
         to_other.wait_send()
@@ -297,49 +316,40 @@
         all_of(cho.at[pl.ds(1, NX - 1)], gat_send.at[2], gat_recv.at[2]).wait_send()
         all_of(stats.at[pl.ds(1, PLANE - 1)], st_send, st_recv).wait_send()
         all_of(fin.at[pl.ds(1, NX - 1)], fin_send, fin_recv).wait_send()
-        all_of(rs_in, rs_send, rs_recv).wait_send()
-        ag_local.wait()
-        out_cg.wait()
+        all_of(rs_in.at[pl.ds(1, PLANE - 1)], rs_send, rs_recv).wait_send()
 
     with jax.named_scope("ag_wait"):
-        all_of(rs_in, ag_send, ag_recv).wait_send()
-        all_of(rs_in, ag_send, ag_recv).wait_recv()
-
-
-def finish(ag, cg, lg_out, cg_out, ag_v, lg_v, cg_v, sem):
-    load = pltpu.make_async_copy(ag, ag_v, sem.at[0])
-    load.start()
-    n = cg_v.shape[0]
-    pieces = [pl.ds(k * (HALF // n), HALF // n) for k in range(n)]
-    moves = [pltpu.make_async_copy(cg.at[p], cg_v.at[k], sem.at[2 + k]) for k, p in enumerate(pieces)]
-    for move in moves:
-        move.start()
-    load.wait()
-    full = ag_v[...].astype(F32)
+        all_of(ag.at[pl.ds(0, PLANE - 1)], ag_send, ag_recv).wait_send()
+        all_of(ag.at[pl.ds(0, PLANE - 1)], ag_send, ag_recv).wait_recv()
+
+
+def finish(ag, cg, lg_out, cg_out, lg_v, sem):
+    move = pltpu.make_async_copy(cg, cg_out, sem.at[0])
+    move.start()
+    full = ag[...].astype(F32)
     lg_v[pl.ds(0, 128), :] = full[:, :8, :].reshape(D, 128).T
     lg_v[pl.ds(128, 128), :] = full[:, 8:, :].reshape(D, 128).T
     store = pltpu.make_async_copy(lg_v, lg_out, sem.at[1])
     store.start()
-    stores = [pltpu.make_async_copy(cg_v.at[k], cg_out.at[p], sem.at[2 + n + k]) for k, p in enumerate(pieces)]
-    for move, out in zip(moves, stores):
+    with jax.named_scope("store_latent"):
+        store.wait()
+    with jax.named_scope("store_code"):
         move.wait()
-        out.start()
-    store.wait()
-    for out in stores:
-        out.wait()
 
 
 def shards(latents, codebook, cotangent, chosen):
     any_space = pl.BlockSpec(memory_space=pl.ANY)
+    vmem = pl.BlockSpec(memory_space=pltpu.VMEM)
     dma = pltpu.SemaphoreType.DMA
+    args = [
+        pltpu.with_memory_space_constraint(v, pltpu.HBM)
+        for v in (latents, cotangent, chosen.reshape(1, T), codebook)
+    ]
     gathered, code_grad = pl.pallas_call(
         kernel,
-        out_shape=(
-            jax.ShapeDtypeStruct((PLANE, 16, 128), BF16),
-            jax.ShapeDtypeStruct((HALF, D), F32),
-        ),
+        out_shape=(pltpu.VMEM((PLANE, 16, 128), BF16), pltpu.VMEM((HALF, D), F32)),
         in_specs=[any_space] * 4,
-        out_specs=(any_space, any_space),
+        out_specs=(vmem, vmem),
         scratch_shapes=[
             pltpu.VMEM((CODES, D), BF16),
             pltpu.VMEM((NX, T, D), BF16),
@@ -349,47 +359,42 @@
             pltpu.VMEM((CODES, T), F32),
             pltpu.VMEM((NX - 1, OWN, T), F32),
             pltpu.VMEM((NX - 1, OWN, T), F32),
-            pltpu.VMEM((PLANE, 3, 2, 128), F32),
-            pltpu.VMEM((NX, 3, 2, 128), F32),
+            pltpu.VMEM((PLANE, 2, 2, 128), F32),
+            pltpu.VMEM((NX, 2, 2, 128), F32),
             pltpu.VMEM((D, T), F32),
             pltpu.VMEM((D, T), F32),
-            pltpu.VMEM((PLANE, 16, 128), BF16),
-            pltpu.VMEM((PLANE - 1, 16, 128), BF16),
+            pltpu.VMEM((PLANE, 2, 16, 128), BF16),
+            pltpu.VMEM((PLANE, 2, 16, 128), BF16),
+            pltpu.VMEM((PLANE, 2, 2, 128), F32),
             pltpu.VMEM((16, 128), BF16),
             pltpu.VMEM((OWN, D), F32),
             pltpu.VMEM((HALF, D), BF16),
             pltpu.VMEM((HALF, D), BF16),
-            pltpu.VMEM((HALF, D), F32),
             dma((len(PARTS),)),
-            dma((3,)),
+            dma((4,)),
             dma((3,)), dma((3,)),
             dma, dma,
             dma, dma,
             dma, dma,
             dma, dma,
             dma, dma,
-            dma((2,)),
             pltpu.SemaphoreType.REGULAR,
         ],
         compiler_params=pltpu.CompilerParams(
-            collective_id=0, has_side_effects=True, vmem_limit_bytes=56 * 2**20
+            collective_id=0, has_side_effects=True, vmem_limit_bytes=42 * 2**20
         ),
         cost_estimate=pl.CostEstimate(
             flops=20 * T * D * CODES, bytes_accessed=8 * 2**20, transcendentals=2 * T * CODES
         ),
-    )(latents, cotangent, chosen.reshape(1, T), codebook)
+    )(*args)
     return pl.pallas_call(
         finish,
         out_shape=(jax.ShapeDtypeStruct((T, D), F32), jax.ShapeDtypeStruct((HALF, D), F32)),
-        in_specs=[any_space] * 2,
+        in_specs=[vmem, vmem],
         out_specs=(any_space, any_space),
-        scratch_shapes=[
-            pltpu.VMEM((PLANE, 16, 128), BF16),
-            pltpu.VMEM((T, D), F32),
-            pltpu.VMEM((4, HALF // 4, D), F32),
-            dma((10,)),
-        ],
-    )(gathered, code_grad)
+        scratch_shapes=[pltpu.VMEM((T, D), F32), dma((2,))],
+        compiler_params=pltpu.CompilerParams(vmem_limit_bytes=4 * 2**20),
+    )(*[pltpu.with_memory_space_constraint(v, pltpu.VMEM) for v in (gathered, code_grad)])
 
 
 def solution(mesh):

time: 34.1 us -> 30.6 us (0.90)
  Pallas kernels: 33.2 us -> 29.9 us
    pallas_call x1, Pallas kernels: 31.1 us -> 28.9 us  [shards(): pl.pallas_call(kernel, out_shape=(pltpu.VMEM((PLANE, 16, 128), BF16), plt...]
    pallas_call x1, Pallas kernels: 2.14 us -> 1.07 us  [shards(): pl.pallas_call(finish, out_shape=(jax.ShapeDtypeStruct((T, D), F32), jax....]
where the time goes in v2:
time: 30.6 us
  Pallas kernels  29.9 us (98%)
  between operations  0.64 us (2%)
    pallas_call x1, Pallas kernels, shards(): pl.pallas_call(kernel, out_shape=(pltpu.VMEM((PLANE, 16, 128), BF16), plt...  28.9 us
    pallas_call x1, Pallas kernels, shards(): pl.pallas_call(finish, out_shape=(jax.ShapeDtypeStruct((T, D), F32), jax....  1.07 us

profile of v2, /device:TPU:2, one launch (start us, length us, event | category | flops | bytes accessed | tf_op | source)
XLA Modules:
  0.0 30.6 jit_solution(13510245292521635694)
XLA Ops:
  0.6 28.9 %shard_map.59 = (bf16[32,16,128]{2,1,0:T(8,128)(2,1)S(1)}, f32[1024,256]{1,0:T(8,128)S(1)}) custom-call(bf16[256,256]{1,0:T(8,128)(2,1)} %lat_hbm.1, bf16[256,256]{1,0:T(8,128)(2,1)} %cot_hbm.1, s32[1,256]{1,0:T(1,128)} %bitcast.1, bf16[8192,256]{1,0:T(8,128)(2,1)} %cb_hbm.1), custom_call_target="tpu_custom_call" | custom-call | flops 10737418240 | bytes 8388608 | tf_op jit(solution)/shard_map/pallas_call | solution.py:348
  29.5 1.1 %shard_map.60 = (f32[256,256]{1,0:T(8,128)}, f32[1024,256]{1,0:T(8,128)}) custom-call(bf16[32,16,128]{2,1,0:T(8,128)(2,1)S(1)} %get-tuple-element.4.ag, f32[1024,256]{1,0:T(8,128)S(1)} %get-tuple-element.5.cg), custom_call_target="tpu_custom_call" | custom-call | tf_op jit(solution)/shard_map/pallas_call | solution.py:390

commit v3 on v2

--- a/solution.py
+++ b/solution.py
@@ -18,10 +18,11 @@
 
 SHIFTS = sorted(
     ((dy, dz) for dy in range(NY) for dz in range(NZ) if (dy, dz) != (0, 0)),
-    key=lambda s: -(min(s[0], NY - s[0]) + min(s[1], NZ - s[1])),
+    key=lambda s: (-min(s[1], NZ - s[1]), -min(s[0], NY - s[0])),
 )
 LOG2E = 1.4426950408889634
 PARTS = (1024, 3072, 4096)
+HALF_STEP = 512
 STEP = 1024
 
 
@@ -43,6 +44,12 @@
 
 def pair(v):
     return jnp.concatenate([v[:, :128], v[:, 128:]], axis=0)
+
+
+def chunks(v):
+    return jnp.concatenate(
+        [v[:, :128].reshape(PLANE, 8, 128), v[:, 128:].reshape(PLANE, 8, 128)], axis=1
+    ).astype(BF16)
 
 
 def fold8(v):
@@ -65,13 +72,14 @@
     cb, lat, cot, cho, lq, uu, lb, ub, stats, fin, acc_a, acc_b,
     rs_out, rs_in, coef, ag_own, cacc, cx_out, cx_in,
     cb_sem, own_sem, gat_send, gat_recv, st_send, st_recv, fin_send, fin_recv,
-    rs_send, rs_recv, ag_send, ag_recv, cx_send, cx_recv, ready_sem,
+    rs_send, rs_recv, ag_send, ag_recv, cx_send, cx_recv, ready_sem, far_sem,
 ):
     tok, code = lax.axis_index("tok"), lax.axis_index("code")
     x, c = tok >> 1, tok & 1
     y, z = code >> 3, code & (NZ - 1)
 
     x_peers = [((((x + d) & (NX - 1)) << 1) + c, code) for d in range(1, NX)]
+    x_right, x_left = x_peers[0], x_peers[2]
     plane_codes = [(((y + dy) & (NY - 1)) << 3) + ((z + dz) & (NZ - 1)) for dy, dz in SHIFTS]
     plane = [(tok, p) for p in plane_codes]
     other = (tok ^ 1, code)
@@ -111,7 +119,7 @@
 
     with jax.named_scope("greet"):
         barrier = pltpu.get_barrier_semaphore()
-        near = x_peers + [other]
+        near = [x_right, x_left, other]
         for p in near:
             pl.semaphore_signal(barrier, inc=1, device_id=p, device_id_type=MESH)
         lax.fori_loop(rank + 1, PLANE, tell(barrier), 0)
@@ -120,10 +128,12 @@
         loads[k].wait()
 
         def step(j, top):
-            rows = pl.ds(pl.multiple_of(starts[k] + j * STEP, STEP), STEP)
-            scores = nt(cb[rows, :], lat[0]) * LOG2E
-            lq[rows, :] = scores
-            return jnp.maximum(top, jnp.max(fold8(scores), axis=0))
+            for i in range(2):
+                rows = pl.ds(pl.multiple_of(starts[k] + j * STEP + i * HALF_STEP, HALF_STEP), HALF_STEP)
+                scores = nt(cb[rows, :], lat[0]) * LOG2E
+                lq[rows, :] = scores
+                top = jnp.maximum(top, jnp.max(fold8(scores), axis=0))
+            return top
 
         return lax.fori_loop(0, PARTS[k] // STEP, step, top, unroll=True)
 
@@ -135,12 +145,19 @@
 
     with jax.named_scope("entry"):
         pl.semaphore_wait(barrier, len(near) + rank)
-    for d in (2, 1, 3):
-        to = x_peers[d - 1]
-        remote(lat_hbm, lat.at[d], gat_send.at[0], gat_recv.at[0], to).start()
-        remote(cot_hbm, cot.at[d], gat_send.at[1], gat_recv.at[1], to).start()
-        remote(cho_hbm, cho.at[d], gat_send.at[2], gat_recv.at[2], to).start()
+    arrays = ((lat_hbm, lat), (cot_hbm, cot), (cho_hbm, cho))
+    to_right = [remote(v, w.at[1], gat_send.at[i], gat_recv.at[i], x_right) for i, (v, w) in enumerate(arrays)]
+    to_left = [remote(v, w.at[3], gat_send.at[3 + i], gat_recv.at[3 + i], x_left) for i, (v, w) in enumerate(arrays)]
+    passed = [
+        remote(lat.at[1], lat.at[2], gat_send.at[6], gat_recv.at[6], x_right),
+        remote(cot.at[3], cot.at[2], gat_send.at[7], gat_recv.at[7], x_left),
+        remote(cho.at[3], cho.at[2], gat_send.at[8], gat_recv.at[8], x_left),
+    ]
+    for copy in (to_right[0], to_left[1], to_left[2], to_right[1], to_left[0], to_right[2]):
+        copy.start()
+    pl.semaphore_signal(far_sem, inc=1, device_id=x_right, device_id_type=MESH)
     lax.fori_loop(0, rank, tell(ready_sem), 0)
+    late = z >= NZ // 2
 
     with jax.named_scope("logits_rest"):
         top8 = logits(2, top8)
@@ -179,7 +196,7 @@
         for k, p in enumerate(plane):
             remote(stats.at[0], stats.at[k + 1], st_send, st_recv, p).start()
 
-    pl.when(z >= NZ // 2)(send_stats)
+    pl.when(late)(send_stats)
 
     with jax.named_scope("sums"):
         acc_a[...] = jnp.zeros_like(acc_a)
@@ -194,17 +211,20 @@
             return carry
 
         lax.fori_loop(0, CODES // STEP, sums_step, 0, unroll=True)
-
         for i, acc in enumerate((acc_a, acc_b)):
-            whole = acc[...] * (1.0 / total)
-            rs_out[:, i] = jnp.concatenate(
-                [whole[:, :128].reshape(PLANE, 8, 128), whole[:, 128:].reshape(PLANE, 8, 128)], axis=1
-            ).astype(BF16)
-    pl.when(z < NZ // 2)(send_stats)
+            rs_out[:, i] = chunks(acc[...] * (1.0 / total))
+    pl.when(jnp.logical_not(late))(send_stats)
     for k, p in enumerate(plane):
         remote(rs_out.at[plane_codes[k]], rs_in.at[k + 1], rs_send, rs_recv, p).start()
     rs_local = pltpu.make_async_copy(rs_out.at[code], rs_in.at[0], own_sem.at[3])
     rs_local.start()
+    with jax.named_scope("forward"):
+        to_right[0].wait_recv()
+        passed[0].start()
+        to_left[1].wait_recv()
+        passed[1].start()
+        to_left[2].wait_recv()
+        passed[2].start()
 
     with jax.named_scope("stats_wait"):
         all_of(stats.at[pl.ds(1, PLANE - 1)], st_send, st_recv).wait_recv()
@@ -222,6 +242,8 @@
         coef[:, 1] = weights * (mean - inners)
         own_scale = row(weights[0]) * (1.0 / total)
         own_inner = row(mean)
+    with jax.named_scope("far"):
+        pl.semaphore_wait(far_sem, 1)
     for d in (2, 1, 3):
         remote(fin.at[0], fin.at[d], fin_send, fin_recv, x_peers[d - 1]).start()
 
@@ -229,9 +251,8 @@
 
     def scores_of_codes():
         with jax.named_scope("gather_wait"):
-            all_of(lat.at[pl.ds(1, NX - 1)], gat_send.at[0], gat_recv.at[0]).wait_recv()
-            all_of(cot.at[pl.ds(1, NX - 1)], gat_send.at[1], gat_recv.at[1]).wait_recv()
-            all_of(cho.at[pl.ds(1, NX - 1)], gat_send.at[2], gat_recv.at[2]).wait_recv()
+            for copy in to_left[:1] + to_right[1:] + passed:
+                copy.wait_recv()
         with jax.named_scope("code_scores"):
             codes = pl.ds(base, OWN)
             for g in range(1, NX):
@@ -250,7 +271,7 @@
 
             lax.fori_loop(0, OWN // ROWS, chosen_step, 0, unroll=True)
 
-    pl.when(z < NZ // 2 - 1)(scores_of_codes)
+    pl.when(z < 2)(scores_of_codes)
 
     with jax.named_scope("rs_wait"):
         rs_local.wait()
@@ -270,7 +291,7 @@
     lax.fori_loop(0, rank, ag_to, 0)
     lax.fori_loop(rank + 1, PLANE, ag_to, 0)
 
-    pl.when(z >= NZ // 2 - 1)(scores_of_codes)
+    pl.when(z >= 2)(scores_of_codes)
 
     with jax.named_scope("fin_wait"):
         all_of(fin.at[pl.ds(1, NX - 1)], fin_send, fin_recv).wait_recv()
@@ -311,9 +332,8 @@
 
     with jax.named_scope("drain"):
         to_other.wait_send()
-        all_of(lat.at[pl.ds(1, NX - 1)], gat_send.at[0], gat_recv.at[0]).wait_send()
-        all_of(cot.at[pl.ds(1, NX - 1)], gat_send.at[1], gat_recv.at[1]).wait_send()
-        all_of(cho.at[pl.ds(1, NX - 1)], gat_send.at[2], gat_recv.at[2]).wait_send()
+        for copy in to_right + to_left + passed:
+            copy.wait_send()
         all_of(stats.at[pl.ds(1, PLANE - 1)], st_send, st_recv).wait_send()
         all_of(fin.at[pl.ds(1, NX - 1)], fin_send, fin_recv).wait_send()
         all_of(rs_in.at[pl.ds(1, PLANE - 1)], rs_send, rs_recv).wait_send()
@@ -372,12 +392,13 @@
             pltpu.VMEM((HALF, D), BF16),
             dma((len(PARTS),)),
             dma((4,)),
-            dma((3,)), dma((3,)),
+            dma((9,)), dma((9,)),
             dma, dma,
             dma, dma,
             dma, dma,
             dma, dma,
             dma, dma,
+            pltpu.SemaphoreType.REGULAR,
             pltpu.SemaphoreType.REGULAR,
         ],
         compiler_params=pltpu.CompilerParams(

time: 30.6 us -> 30.6 us (level)
  no operation moved by 1% of the time
where the time goes in v3:
time: 30.6 us; the launch traced here: 30.5 us
  Pallas kernels  29.9 us (98%)
  between operations  0.64 us (2%)
    pallas_call x1, Pallas kernels, shards(): pl.pallas_call(kernel, out_shape=(pltpu.VMEM((PLANE, 16, 128), BF16), plt...  28.8 us
    pallas_call x1, Pallas kernels, shards(): pl.pallas_call(finish, out_shape=(jax.ShapeDtypeStruct((T, D), F32), jax....  1.07 us

profile of v3, /device:TPU:2, one launch (start us, length us, event | category | flops | bytes accessed | tf_op | source)
XLA Modules:
  0.0 30.5 jit_solution(14037755427880383817)
XLA Ops:
  0.6 28.8 %shard_map.59 = (bf16[32,16,128]{2,1,0:T(8,128)(2,1)S(1)}, f32[1024,256]{1,0:T(8,128)S(1)}) custom-call(bf16[256,256]{1,0:T(8,128)(2,1)} %lat_hbm.1, bf16[256,256]{1,0:T(8,128)(2,1)} %cot_hbm.1, s32[1,256]{1,0:T(1,128)} %bitcast.1, bf16[8192,256]{1,0:T(8,128)(2,1)} %cb_hbm.1), custom_call_target="tpu_custom_call" | custom-call | flops 10737418240 | bytes 8388608 | tf_op jit(solution)/shard_map/pallas_call | solution.py:368
  29.5 1.1 %shard_map.60 = (f32[256,256]{1,0:T(8,128)}, f32[1024,256]{1,0:T(8,128)}) custom-call(bf16[32,16,128]{2,1,0:T(8,128)(2,1)S(1)} %get-tuple-element.4.ag, f32[1024,256]{1,0:T(8,128)S(1)} %get-tuple-element.5.cg), custom_call_target="tpu_custom_call" | custom-call | tf_op jit(solution)/shard_map/pallas_call | solution.py:411

commit v4 on v2

--- a/solution.py
+++ b/solution.py
@@ -324,17 +324,20 @@
 
 
 def finish(ag, cg, lg_out, cg_out, lg_v, sem):
-    move = pltpu.make_async_copy(cg, cg_out, sem.at[0])
-    move.start()
+    moves = []
+    for k in range(8):
+        piece = pl.ds(k * (HALF // 8), HALF // 8)
+        moves.append(pltpu.make_async_copy(cg.at[piece], cg_out.at[piece], sem.at[k]))
+        moves[-1].start()
     full = ag[...].astype(F32)
-    lg_v[pl.ds(0, 128), :] = full[:, :8, :].reshape(D, 128).T
-    lg_v[pl.ds(128, 128), :] = full[:, 8:, :].reshape(D, 128).T
-    store = pltpu.make_async_copy(lg_v, lg_out, sem.at[1])
-    store.start()
-    with jax.named_scope("store_latent"):
-        store.wait()
-    with jax.named_scope("store_code"):
-        move.wait()
+    for k in range(2):
+        piece = pl.ds(k * 128, 128)
+        lg_v[piece, :] = full[:, k * 8 : k * 8 + 8, :].reshape(D, 128).T
+        moves.append(pltpu.make_async_copy(lg_v.at[piece], lg_out.at[piece], sem.at[8 + k]))
+        moves[-1].start()
+    with jax.named_scope("stores"):
+        for move in moves:
+            move.wait()
 
 
 def shards(latents, codebook, cotangent, chosen):
@@ -392,7 +395,7 @@
         out_shape=(jax.ShapeDtypeStruct((T, D), F32), jax.ShapeDtypeStruct((HALF, D), F32)),
         in_specs=[vmem, vmem],
         out_specs=(any_space, any_space),
-        scratch_shapes=[pltpu.VMEM((T, D), F32), dma((2,))],
+        scratch_shapes=[pltpu.VMEM((T, D), F32), dma((10,))],
         compiler_params=pltpu.CompilerParams(vmem_limit_bytes=4 * 2**20),
     )(*[pltpu.with_memory_space_constraint(v, pltpu.VMEM) for v in (gathered, code_grad)])
 

time: 30.6 us -> 30.7 us (level)
  no operation moved by 1% of the time
where the time goes in v4:
time: 30.7 us; the launch traced here: 30.6 us
  Pallas kernels  30 us (98%)
  between operations  0.64 us (2%)
    pallas_call x1, Pallas kernels, shards(): pl.pallas_call(kernel, out_shape=(pltpu.VMEM((PLANE, 16, 128), BF16), plt...  28.9 us
    pallas_call x1, Pallas kernels, shards(): pl.pallas_call(finish, out_shape=(jax.ShapeDtypeStruct((T, D), F32), jax....  1.13 us

profile of v4, /device:TPU:2, one launch (start us, length us, event | category | flops | bytes accessed | tf_op | source)
XLA Modules:
  0.0 30.6 jit_solution(17945688494481670330)
XLA Ops:
  0.6 28.9 %shard_map.59 = (bf16[32,16,128]{2,1,0:T(8,128)(2,1)S(1)}, f32[1024,256]{1,0:T(8,128)S(1)}) custom-call(bf16[256,256]{1,0:T(8,128)(2,1)} %lat_hbm.1, bf16[256,256]{1,0:T(8,128)(2,1)} %cot_hbm.1, s32[1,256]{1,0:T(1,128)} %bitcast.1, bf16[8192,256]{1,0:T(8,128)(2,1)} %cb_hbm.1), custom_call_target="tpu_custom_call" | custom-call | flops 10737418240 | bytes 8388608 | tf_op jit(solution)/shard_map/pallas_call | solution.py:351
  29.5 1.1 %shard_map.60 = (f32[256,256]{1,0:T(8,128)}, f32[1024,256]{1,0:T(8,128)}) custom-call(bf16[32,16,128]{2,1,0:T(8,128)(2,1)S(1)} %get-tuple-element.4.ag, f32[1024,256]{1,0:T(8,128)S(1)} %get-tuple-element.5.cg), custom_call_target="tpu_custom_call" | custom-call | tf_op jit(solution)/shard_map/pallas_call | solution.py:393
